TPU v7x, 512 devices: a whole 4x8x8 slice. The times are simulated.
512 devices in a mesh: expert: 64 (over x, z, core), tensor: 8 (over y).
Axes of the slice: x: 4, y: 8, z: 8, core: 2. Of those that a mesh axis runs over, the one named last changes fastest.
Arguments:
- tokens: bfloat16 [8192, 2048], P('expert', 'tensor'), may hold values from -6 to 6
- cotangent: bfloat16 [8192, 2048], P('expert', 'tensor'), may hold values from -6 to 6
- route_ids: int32 [8192, 6], P('expert'), may hold values from 0 to 63, all different within a row
- route_weights: float32 [8192, 6], P('expert'), may hold values from 0.05 to 0.5
- shared_gate: bfloat16 [1408, 2048], P('tensor'), may hold values from -0.125 to 0.125
- shared_up: bfloat16 [1408, 2048], P('tensor'), may hold values from -0.125 to 0.125
- shared_down: bfloat16 [1408, 2048], P('tensor'), may hold values from -0.15625 to 0.15625
- expert_gate: bfloat16 [64, 1408, 2048], P('expert', 'tensor'), may hold values from -0.125 to 0.125
- expert_up: bfloat16 [64, 1408, 2048], P('expert', 'tensor'), may hold values from -0.125 to 0.125
- expert_down: bfloat16 [64, 1408, 2048], P('expert', 'tensor'), may hold values from -0.15625 to 0.15625
Outputs:
- layer_output: bfloat16 [8192, 2048], P('expert', 'tensor')
- input_grad: bfloat16 [8192, 2048], P('expert', 'tensor')
Inputs may be any that keep to these rules, and one draw needn't show every extreme that they name: `route_ids`: each row names 6 different experts.
All inputs are finite; a program needn't handle non-finite values.
Results may differ from a plain program's by a relative error of at most 0.0051.
Values may be sent and summed in bfloat16 or wider, within the bound.
A program may use at most 64 MiB of HBM per device.

v0:
```python
import jax
import jax.numpy as jnp
from jax import lax
from jax.sharding import PartitionSpec as P


def silu_parts(pre_act):
    sigmoid_value = jax.nn.sigmoid(pre_act)
    return (pre_act * sigmoid_value, sigmoid_value * (1.0 + pre_act * (1.0 - sigmoid_value)))


def on_device(
    tokens,
    cotangent,
    route_ids,
    route_weights,
    shared_gate,
    shared_up,
    shared_down,
    expert_gate,
    expert_up,
    expert_down,
):
    expert_count = lax.axis_size("expert")
    tok_rows, top_count = route_ids.shape
    local_experts = expert_gate.shape[0]
    all_experts = local_experts * expert_count
    capacity = tok_rows * top_count // (2 * all_experts)
    slot_total = all_experts * capacity
    flat_ids = route_ids.reshape(-1)
    one_hot = (flat_ids[:, None] == jnp.arange(all_experts, dtype=jnp.int32)[None, :]).astype(
        jnp.int32
    )
    rank_in = jnp.sum((jnp.cumsum(one_hot, axis=0) - one_hot) * one_hot, axis=1)
    kept_mask = rank_in < capacity
    slot_index = jnp.where(kept_mask, flat_ids * capacity + rank_in, slot_total)
    slot_match = jnp.arange(slot_total, dtype=jnp.int32)[:, None] == slot_index[None, :]
    dispatch = jnp.any(slot_match.reshape(slot_total, tok_rows, top_count), axis=2).astype(
        jnp.bfloat16
    )
    gate_flat = route_weights.reshape(-1)
    slot_gate = jnp.sum(jnp.where(slot_match, gate_flat[None, :], 0.0), axis=1)
    gate_dispatch = dispatch.astype(jnp.float32) * slot_gate[:, None]
    x_full, c_full = (
        lax.all_gather(tokens, "tensor", axis=1, tiled=True),
        lax.all_gather(cotangent, "tensor", axis=1, tiled=True),
    )
    x_slots = jnp.dot(dispatch, x_full, preferred_element_type=jnp.float32).astype(jnp.bfloat16)
    g_slots = (
        slot_gate[:, None] * jnp.dot(dispatch, c_full, preferred_element_type=jnp.float32)
    ).astype(jnp.bfloat16)
    x_recv, g_recv = (
        lax.all_to_all(x_slots, "expert", split_axis=0, concat_axis=0, tiled=True),
        lax.all_to_all(g_slots, "expert", split_axis=0, concat_axis=0, tiled=True),
    )

    def owner_layout(values):
        shaped = values.reshape(expert_count, local_experts, capacity, values.shape[-1])
        return shaped.transpose(1, 0, 2, 3).reshape(
            local_experts, expert_count * capacity, values.shape[-1]
        )

    def source_layout(values):
        shaped = values.reshape(local_experts, expert_count, capacity, values.shape[-1])
        return shaped.transpose(1, 0, 2, 3).reshape(slot_total, values.shape[-1])

    x_own = owner_layout(x_recv)
    g_own = owner_layout(g_recv)
    gate_pre = jnp.einsum("erd,efd->erf", x_own, expert_gate, preferred_element_type=jnp.float32)
    up_pre = jnp.einsum("erd,efd->erf", x_own, expert_up, preferred_element_type=jnp.float32)
    act_value, act_slope = silu_parts(gate_pre)
    hidden = (act_value * up_pre).astype(jnp.bfloat16)
    grad_hidden = jnp.einsum("erd,efd->erf", g_own, expert_down, preferred_element_type=jnp.float32)
    grad_gate = (grad_hidden * up_pre * act_slope).astype(jnp.bfloat16)
    grad_up = (grad_hidden * act_value).astype(jnp.bfloat16)
    value_part = source_layout(
        jnp.einsum("erf,efd->erd", hidden, expert_down, preferred_element_type=jnp.float32).astype(
            jnp.bfloat16
        )
    )
    grads_joined = jnp.concatenate((grad_gate, grad_up), axis=2)
    weights_joined = jnp.concatenate((expert_gate, expert_up), axis=1)
    input_term = jnp.einsum(
        "erf,efd->erd", grads_joined, weights_joined, preferred_element_type=jnp.float32
    )
    input_part = source_layout(input_term.astype(jnp.bfloat16))
    shared_gate_pre = jnp.einsum(
        "td,fd->tf", x_full, shared_gate, preferred_element_type=jnp.float32
    )
    shared_up_pre = jnp.einsum("td,fd->tf", x_full, shared_up, preferred_element_type=jnp.float32)
    shared_act, shared_slope = silu_parts(shared_gate_pre)
    shared_hidden = (shared_act * shared_up_pre).astype(jnp.bfloat16)
    shared_value = jnp.dot(shared_hidden, shared_down, preferred_element_type=jnp.float32)
    shared_grad_hidden = jnp.einsum(
        "td,fd->tf", c_full, shared_down, preferred_element_type=jnp.float32
    )
    shared_grad_gate = (shared_grad_hidden * shared_up_pre * shared_slope).astype(jnp.bfloat16)
    shared_grad_up = (shared_grad_hidden * shared_act).astype(jnp.bfloat16)
    shared_input = jnp.dot(shared_grad_gate, shared_gate, preferred_element_type=jnp.float32)
    shared_input = shared_input + jnp.dot(
        shared_grad_up, shared_up, preferred_element_type=jnp.float32
    )
    value_back, input_back = (
        lax.all_to_all(value_part, "expert", split_axis=0, concat_axis=0, tiled=True),
        lax.all_to_all(input_part, "expert", split_axis=0, concat_axis=0, tiled=True),
    )
    early_value = shared_value + jnp.einsum(
        "st,sd->td",
        gate_dispatch,
        value_back.astype(jnp.float32),
        precision=lax.Precision.HIGHEST,
        preferred_element_type=jnp.float32,
    )
    early_input = shared_input + jnp.einsum(
        "st,sd->td",
        dispatch,
        input_back,
        precision=lax.Precision.HIGHEST,
        preferred_element_type=jnp.float32,
    )
    value_total, input_total = (
        lax.psum_scatter(early_value, "tensor", scatter_dimension=1, tiled=True),
        lax.psum_scatter(early_input, "tensor", scatter_dimension=1, tiled=True),
    )
    return (value_total.astype(jnp.bfloat16), input_total.astype(jnp.bfloat16))


def solution(mesh):
    in_specs = (
        P("expert", "tensor"),
        P("expert", "tensor"),
        P("expert", None),
        P("expert", None),
        P("tensor", None),
        P("tensor", None),
        P("tensor", None),
        P("expert", "tensor", None),
        P("expert", "tensor", None),
        P("expert", "tensor", None),
    )
    out_specs = (P("expert", "tensor"), P("expert", "tensor"))
    return jax.shard_map(
        on_device, mesh=mesh, in_specs=in_specs, out_specs=out_specs, check_vma=False
    )
```

profile of v0, /device:TPU:2, one launch (start us, length us, event | category | flops | bytes accessed | tf_op | source)
XLA Modules:
  0.0 333.4 jit_solution(1822526318146382311)
XLA Ops:
  9.0 27.1 %all_gather.6 = bf16[128,2048]{1,0:T(8,128)(2,1)S(1)} all-gather(bf16[128,256]{1,0:T(8,128)(2,1)} %param.10), channel_id=1, replica_groups=mesh['expert'=64,'tensor'=8] {'tensor'}, dimensions={1}, use_global_device_ids=true | all-gather | bytes 589824 | tf_op jit(solution)/shard_map/all_gather | solution.py:45
  36.3 1.8 reduce-window.6
  39.5 1.6 all_to_all.32
  41.1 14.0 %all-to-all-start = ((bf16[64,6,2048]{2,1,0:T(8,128)(2,1)}), bf16[64,6,2048]{2,1,0:T(8,128)(2,1)S(1)}, u32[]{:S(2)}, u32[]{:S(2)}) async-start(bf16[64,6,2048]{2,1,0:T(8,128)(2,1)} %all_to_all.32), calls=%async_computation | async-start | bytes 4194304 | tf_op jit(solution)/shard_map/all_to_all | solution.py:53
  55.6 25.5 %all_gather.7 = bf16[128,2048]{1,0:T(8,128)(2,1)S(1)} all-gather(bf16[128,256]{1,0:T(8,128)(2,1)S(1)} %copy-done.14), channel_id=1, replica_groups=mesh['expert'=64,'tensor'=8] {'tensor'}, dimensions={1}, use_global_device_ids=true | all-gather | bytes 589824 | tf_op jit(solution)/shard_map/all_gather | solution.py:46
  81.9 1.7 multiply_convert_fusion
  83.6 3.7 %all_to_all.38 = bf16[64,6,2048]{2,1,0:T(8,128)(2,1)} reshape(bf16[384,2048]{1,0:T(8,128)(2,1)} %multiply_convert_fusion) | data formatting | bytes 3145728 | tf_op jit(solution)/shard_map/all_to_all | solution.py:54
  87.3 17.3 %all-to-all-done = bf16[64,6,2048]{2,1,0:T(8,128)(2,1)S(1)} async-done(((bf16[64,6,2048]{2,1,0:T(8,128)(2,1)}), bf16[64,6,2048]{2,1,0:T(8,128)(2,1)S(1)}, u32[]{:S(2)}, u32[]{:S(2)}) %all-to-all-start) | async-done | bytes 1572896 | tf_op jit(solution)/shard_map/all_to_all | solution.py:53
  105.9 7.7 %all-to-all-start.2 = ((bf16[64,6,2048]{2,1,0:T(8,128)(2,1)}), bf16[64,6,2048]{2,1,0:T(8,128)(2,1)}, u32[]{:S(2)}, u32[]{:S(2)}) async-start(bf16[64,6,2048]{2,1,0:T(8,128)(2,1)} %all_to_all.38), calls=%async_computation.3 | async-start | bytes 4194304 | tf_op jit(solution)/shard_map/all_to_all | solution.py:54
  113.6 2.6 all_to_all.34
  116.3 1.8 fusion.6
  121.7 41.4 %all-to-all-done.2 = bf16[64,6,2048]{2,1,0:T(8,128)(2,1)} async-done(((bf16[64,6,2048]{2,1,0:T(8,128)(2,1)}), bf16[64,6,2048]{2,1,0:T(8,128)(2,1)}, u32[]{:S(2)}, u32[]{:S(2)}) %all-to-all-start.2) | async-done | bytes 1572896 | tf_op jit(solution)/shard_map/all_to_all | solution.py:54
  163.1 7.5 %all-to-all-start.1 = ((bf16[64,6,2048]{2,1,0:T(8,128)(2,1)}), bf16[64,6,2048]{2,1,0:T(8,128)(2,1)S(1)}, u32[]{:S(2)}, u32[]{:S(2)}) async-start(bf16[64,6,2048]{2,1,0:T(8,128)(2,1)} %all_to_all.35), calls=%async_computation.1 | async-start | bytes 4194304 | tf_op jit(solution)/shard_map/all_to_all | solution.py:104
  170.6 3.7 %all_to_all.40 = bf16[384,2048]{1,0:T(8,128)(2,1)} reshape(bf16[64,6,2048]{2,1,0:T(8,128)(2,1)} %all-to-all-done.2) | data formatting | bytes 3145728 | tf_op jit(solution)/shard_map/all_to_all | solution.py:54
  174.4 2.3 fusion.20
  176.7 2.2 convolution_convert_fusion.1
  178.9 3.7 %all_to_all.41 = bf16[64,6,2048]{2,1,0:T(8,128)(2,1)} reshape(bf16[384,2048]{1,0:T(8,128)(2,1)} %convolution_convert_fusion.1) | data formatting | bytes 3145728 | tf_op jit(solution)/shard_map/all_to_all | solution.py:105
  182.5 37.6 %all-to-all-done.1 = bf16[64,6,2048]{2,1,0:T(8,128)(2,1)S(1)} async-done(((bf16[64,6,2048]{2,1,0:T(8,128)(2,1)}), bf16[64,6,2048]{2,1,0:T(8,128)(2,1)S(1)}, u32[]{:S(2)}, u32[]{:S(2)}) %all-to-all-start.1) | async-done | bytes 1572896 | tf_op jit(solution)/shard_map/all_to_all | solution.py:104
  221.5 7.5 %all-to-all-start.3 = ((bf16[64,6,2048]{2,1,0:T(8,128)(2,1)}), bf16[64,6,2048]{2,1,0:T(8,128)(2,1)S(1)}, u32[]{:S(2)}, u32[]{:S(2)}) async-start(bf16[64,6,2048]{2,1,0:T(8,128)(2,1)} %all_to_all.41), calls=%async_computation.4 | async-start | bytes 4194304 | tf_op jit(solution)/shard_map/all_to_all | solution.py:105
  233.7 3.7 %all_to_all.37 = bf16[384,2048]{1,0:T(8,128)(2,1)} reshape(bf16[64,6,2048]{2,1,0:T(8,128)(2,1)} %copy-done.1) | data formatting | bytes 3145728 | tf_op jit(solution)/shard_map/all_to_all | solution.py:104
  237.4 3.9 %convolution_add_fusion.2 = f32[128,2048]{1,0:T(8,128)} fusion(f32[128,2048]{1,0:T(8,128)} %fusion.25, bf16[384,2048]{1,0:T(8,128)(2,1)} %all_to_all.37, f32[384]{0:T(512)S(1)} %select_reduce_fusion, pred[384,128]{1,0:T(8,128)(4,1)S(1)} %fusion.2), kind=kOutput, calls=%fused_computation.6 | convolution fusion | flops 1208369152 | bytes 3720704 | tf_op jit(solution)/shard_map/st,sd->td/dot_general | solution.py:107
  245.6 33.0 %all-to-all-done.3 = bf16[64,6,2048]{2,1,0:T(8,128)(2,1)S(1)} async-done(((bf16[64,6,2048]{2,1,0:T(8,128)(2,1)}), bf16[64,6,2048]{2,1,0:T(8,128)(2,1)S(1)}, u32[]{:S(2)}, u32[]{:S(2)}) %all-to-all-start.3) | async-done | bytes 1572896 | tf_op jit(solution)/shard_map/all_to_all | solution.py:105
  280.0 3.2 convolution_add_fusion
  284.8 40.3 %reduce-scatter.5.cloned.1.call-done = f32[128,256]{1,0:T(8,128)} async-done(((f32[128,2048]{1,0:T(8,128)}), f32[128,256]{1,0:T(8,128)}) %reduce-scatter.5.cloned.1.call-update) | async-done | bytes 131088 | tf_op jit(solution)/shard_map/reduce_scatter | solution.py:123
  (67 shorter events, 24.2 us)
Async XLA Ops:
  7.2 112.4 %copy-start = (bf16[1,176,2048]{2,1,0:T(8,128)(2,1)S(1)}, bf16[1,176,2048]{2,1,0:T(8,128)(2,1)}, u32[]{:S(2)}) copy-start(bf16[1,176,2048]{2,1,0:T(8,128)(2,1)} %param.19) | copy-start | bytes 2162692
  41.1 14.0 %copy-start.15 = (f32[128,6]{0,1:T(8,128)S(1)}, f32[128,6]{0,1:T(8,128)}, u32[]{:S(2)}) copy-start(f32[128,6]{0,1:T(8,128)} %param.13) | copy-start | bytes 9220
  41.1 14.5 %copy-start.14 = (bf16[128,256]{1,0:T(8,128)(2,1)S(1)}, bf16[128,256]{1,0:T(8,128)(2,1)}, u32[]{:S(2)}) copy-start(bf16[128,256]{1,0:T(8,128)(2,1)} %param.11) | copy-start | bytes 196612
  41.1 63.5 %all-to-all-start = ((bf16[64,6,2048]{2,1,0:T(8,128)(2,1)}), bf16[64,6,2048]{2,1,0:T(8,128)(2,1)S(1)}, u32[]{:S(2)}, u32[]{:S(2)}) async-start(bf16[64,6,2048]{2,1,0:T(8,128)(2,1)} %all_to_all.32), calls=%async_computation | async-start | bytes 4194304 | tf_op jit(solution)/shard_map/all_to_all | solution.py:53
  81.1 0.8 copy-start.3
  104.6 1.3 copy-start.2
  105.9 57.2 %all-to-all-start.2 = ((bf16[64,6,2048]{2,1,0:T(8,128)(2,1)}), bf16[64,6,2048]{2,1,0:T(8,128)(2,1)}, u32[]{:S(2)}, u32[]{:S(2)}) async-start(bf16[64,6,2048]{2,1,0:T(8,128)(2,1)} %all_to_all.38), calls=%async_computation.3 | async-start | bytes 4194304 | tf_op jit(solution)/shard_map/all_to_all | solution.py:54
  116.3 1.9 copy-start.12
  118.1 2.0 copy-start.8
  118.8 0.7 copy-start.9
  163.1 57.1 %all-to-all-start.1 = ((bf16[64,6,2048]{2,1,0:T(8,128)(2,1)}), bf16[64,6,2048]{2,1,0:T(8,128)(2,1)S(1)}, u32[]{:S(2)}, u32[]{:S(2)}) async-start(bf16[64,6,2048]{2,1,0:T(8,128)(2,1)} %all_to_all.35), calls=%async_computation.1 | async-start | bytes 4194304 | tf_op jit(solution)/shard_map/all_to_all | solution.py:104
  174.4 2.3 copy-start.11
  174.4 2.3 copy-start.13
  220.2 1.3 copy-start.1
  221.5 57.1 %all-to-all-start.3 = ((bf16[64,6,2048]{2,1,0:T(8,128)(2,1)}), bf16[64,6,2048]{2,1,0:T(8,128)(2,1)S(1)}, u32[]{:S(2)}, u32[]{:S(2)}) async-start(bf16[64,6,2048]{2,1,0:T(8,128)(2,1)} %all_to_all.41), calls=%async_computation.4 | async-start | bytes 4194304 | tf_op jit(solution)/shard_map/all_to_all | solution.py:105
  229.0 54.2 %reduce-scatter.3.cloned.1.call-start = ((), (), s32[]{:S(2)}) async-start(), calls=%async_computation.6 | async-start | bytes 1179648 | tf_op jit(solution)/shard_map/reduce_scatter | solution.py:122
  229.2 3.1 copy-start.5
  230.8 1.5 copy-start.10
  237.4 3.9 %copy-start.4 = (bf16[128,2048]{1,0:T(8,128)(2,1)S(1)}, bf16[128,2048]{1,0:T(8,128)(2,1)}, u32[]{:S(2)}) copy-start(bf16[128,2048]{1,0:T(8,128)(2,1)} %copy-done.3) | copy-start | bytes 1572868
  241.3 83.8 %reduce-scatter.5.cloned.1.call-start = ((), (), s32[]{:S(2)}) async-start(), calls=%async_computation.7 | async-start | bytes 1179648 | tf_op jit(solution)/shard_map/reduce_scatter | solution.py:123
  241.4 1.6 copy-start.6
  241.4 2.8 copy-start.7
Sparse Core Ops, SparseCore 0:
  241.4 40.5 reduce-scatter.2
  284.8 40.1 reduce-scatter.4
where the time goes:
time: 335 us; the launch traced here: 333 us
  waiting for transfers between devices  170 us (51%)
  blocking collectives  52.6 us (16%)
  starting transfers between devices  37 us (11%)
  local copies, waits for them, and re-layouts  28.1 us (8%)
  matrix products  25.5 us (8%)
  between operations  14.4 us (4%)
  other arithmetic  6.19 us (2%)
    all_to_all x1, waiting for transfers between devices, on_device(): lax.all_to_all(g_slots, 'expert', split_axis=0, concat_axis=0, tiled=True)  41.4 us
    reduce_scatter x1, waiting for transfers between devices, on_device(): lax.psum_scatter(early_input, 'tensor', scatter_dimension=1, tiled=True)  40.3 us
    all_to_all x1, waiting for transfers between devices, on_device(): lax.all_to_all(value_part, 'expert', split_axis=0, concat_axis=0, tiled=T...  37.6 us
    all_to_all x1, waiting for transfers between devices, on_device(): lax.all_to_all(input_part, 'expert', split_axis=0, concat_axis=0, tiled=T...  33 us
    all_gather x1, blocking collectives, on_device(): lax.all_gather(tokens, 'tensor', axis=1, tiled=True)  27.1 us
    all_gather x1, blocking collectives, on_device(): lax.all_gather(cotangent, 'tensor', axis=1, tiled=True)  25.5 us
    all_to_all x1, waiting for transfers between devices, on_device(): lax.all_to_all(x_slots, 'expert', split_axis=0, concat_axis=0, tiled=True)  17.3 us
    all_to_all x1, starting transfers between devices, on_device(): lax.all_to_all(x_slots, 'expert', split_axis=0, concat_axis=0, tiled=True)  14 us
  transfers between devices with their start and end apart: 6, of which 5 were waited for; matrix products, arithmetic and copies ran while one was open for 8% of the time, Pallas kernels for 0%

commit v1 on v0

--- a/solution.py
+++ b/solution.py
@@ -2,6 +2,28 @@
 import jax.numpy as jnp
 from jax import lax
 from jax.sharding import PartitionSpec as P
+
+
+def joined_along(blocks, dim):
+    blocks = jnp.moveaxis(blocks, 0, dim)
+    lengths = blocks.shape
+    return blocks.reshape(*lengths[:dim], lengths[dim] * lengths[dim + 1], *lengths[dim + 2 :])
+
+
+def collect(x, axis, dim):
+    peers = lax.axis_size(axis)
+    pairs = [(i, (i + 1) % peers) for i in range(peers)]
+    back = [(b, a) for a, b in pairs]
+    lower, upper = ([], [])
+    for step in range(peers - 1):
+        if step % 2 == 0:
+            lower.append(lax.ppermute(lower[-1] if lower else x, axis, pairs))
+        else:
+            upper.append(lax.ppermute(upper[-1] if upper else x, axis, back))
+    blocks = jnp.stack([*lower[::-1], x, *upper])
+    shift = lax.axis_index(axis) - len(lower)
+    blocks = blocks[(jnp.arange(peers) - shift) % peers]
+    return joined_along(blocks, dim)
 
 
 def silu_parts(pre_act):
@@ -42,7 +64,7 @@
     slot_gate = jnp.sum(jnp.where(slot_match, gate_flat[None, :], 0.0), axis=1)
     gate_dispatch = dispatch.astype(jnp.float32) * slot_gate[:, None]
     x_full, c_full = (
-        lax.all_gather(tokens, "tensor", axis=1, tiled=True),
+        collect(tokens, "tensor", 1),
         lax.all_gather(cotangent, "tensor", axis=1, tiled=True),
     )
     x_slots = jnp.dot(dispatch, x_full, preferred_element_type=jnp.float32).astype(jnp.bfloat16)

time: 335 us -> 345 us (1.030)
  blocking collectives: 52.6 us -> 26.9 us
  starting transfers between devices: 37 us -> 60.7 us
  waiting for transfers between devices: 170 us -> 180 us
    reduce_scatter x1, waiting for transfers between devices: 40.3 us -> 0.02 us  [on_device(): lax.psum_scatter(early_input, 'tensor', scatter_dimension=1, tiled=True)]
    reduce_scatter x1, waiting for transfers between devices: 0.02 us -> 40 us  [on_device(): lax.psum_scatter(early_value, 'tensor', scatter_dimension=1, tiled=True)]
    all_to_all x1, waiting for transfers between devices: 41.4 us -> 10.2 us  [on_device(): lax.all_to_all(g_slots, 'expert', split_axis=0, concat_axis=0, tiled=True)]
    all_to_all x1, waiting for transfers between devices: 17.3 us -> 48 us  [on_device(): lax.all_to_all(x_slots, 'expert', split_axis=0, concat_axis=0, tiled=True)]
    all_gather x1 -> x0, blocking collectives: 27.1 us -> none  [on_device(): lax.all_gather(tokens, 'tensor', axis=1, tiled=True)]
    ppermute x0 -> x7, starting transfers between devices: none -> 23.9 us  [the longest x3 15.4 us: collect(): upper.append(lax.ppermute(upper[-1] if upper else x, axis, back))]
    all_to_all x1, waiting for transfers between devices: 33 us -> 41.4 us  [on_device(): lax.all_to_all(input_part, 'expert', split_axis=0, concat_axis=0, tiled=T...]
    all_to_all x1, starting transfers between devices: 7.71 us -> 14 us  [on_device(): lax.all_to_all(g_slots, 'expert', split_axis=0, concat_axis=0, tiled=True)]
  transfers between devices with their start and end apart: 6 -> 13, of which waited for: 5 -> 9; matrix products, arithmetic and copies ran while one was open for 8% -> 8% of each run, Pallas kernels for 0% -> 0%
where the time goes in v1:
time: 345 us; the launch traced here: 343 us
  waiting for transfers between devices  180 us (52%)
  starting transfers between devices  60.7 us (18%)
  local copies, waits for them, and re-layouts  30.1 us (9%)
  blocking collectives  26.9 us (8%)
  matrix products  25 us (7%)
  between operations  14.5 us (4%)
  other arithmetic  6.14 us (2%)
    all_to_all x1, waiting for transfers between devices, on_device(): lax.all_to_all(x_slots, 'expert', split_axis=0, concat_axis=0, tiled=True)  48 us
    all_to_all x1, waiting for transfers between devices, on_device(): lax.all_to_all(input_part, 'expert', split_axis=0, concat_axis=0, tiled=T...  41.4 us
    reduce_scatter x1, waiting for transfers between devices, on_device(): lax.psum_scatter(early_value, 'tensor', scatter_dimension=1, tiled=True)  40 us
    all_to_all x1, waiting for transfers between devices, on_device(): lax.all_to_all(value_part, 'expert', split_axis=0, concat_axis=0, tiled=T...  34.7 us
    all_gather x1, blocking collectives, on_device(): lax.all_gather(cotangent, 'tensor', axis=1, tiled=True)  26.9 us
    ppermute x3, starting transfers between devices, collect(): upper.append(lax.ppermute(upper[-1] if upper else x, axis, back))  15.4 us
    all_to_all x1, starting transfers between devices, on_device(): lax.all_to_all(g_slots, 'expert', split_axis=0, concat_axis=0, tiled=True)  14 us
    all_to_all x1, waiting for transfers between devices, on_device(): lax.all_to_all(g_slots, 'expert', split_axis=0, concat_axis=0, tiled=True)  10.2 us
  transfers between devices with their start and end apart: 13, of which 9 were waited for; matrix products, arithmetic and copies ran while one was open for 8% of the time, Pallas kernels for 0%

profile of v1, /device:TPU:2, one launch (start us, length us, event | category | flops | bytes accessed | tf_op | source)
XLA Modules:
  0.0 343.2 jit_solution(1316483135756925290)
XLA Ops:
  12.1 26.9 %all_gather.3 = bf16[128,2048]{1,0:T(8,128)(2,1)S(1)} all-gather(bf16[128,256]{1,0:T(8,128)(2,1)S(1)} %copy-done.15), channel_id=1, replica_groups=mesh['expert'=64,'tensor'=8] {'tensor'}, dimensions={1}, use_global_device_ids=true | all-gather | bytes 589824 | tf_op jit(solution)/shard_map/all_gather | solution.py:68
  42.0 14.0 %all-to-all-start.2 = ((bf16[64,6,2048]{2,1,0:T(8,128)(2,1)}), bf16[64,6,2048]{2,1,0:T(8,128)(2,1)S(1)}, u32[]{:S(2)}, u32[]{:S(2)}) async-start(bf16[64,6,2048]{2,1,0:T(8,128)(2,1)} %all_to_all.38), calls=%async_computation.3 | async-start | bytes 4194304 | tf_op jit(solution)/shard_map/all_to_all | solution.py:76
  56.0 2.7 collective-permute-start
  58.8 4.6 %collective-permute-done = bf16[128,256]{1,0:T(8,128)(2,1)S(1)} collective-permute-done((bf16[128,256]{1,0:T(8,128)(2,1)S(1)}, bf16[128,256]{1,0:T(8,128)(2,1)S(1)}, u32[]{:S(2)}, u32[]{:S(2)}) %collective-permute-start) | collective-permute-done | bytes 65568 | tf_op jit(solution)/shard_map/ppermute | solution.py:20
  65.3 5.1 %collective-permute-start.4 = (bf16[128,256]{1,0:T(8,128)(2,1)S(1)}, bf16[128,256]{1,0:T(8,128)(2,1)S(1)}, u32[]{:S(2)}, u32[]{:S(2)}) collective-permute-start(bf16[128,256]{1,0:T(8,128)(2,1)S(1)} %copy-done.16), channel_id=1, source_target_pairs={{1,0},{2,1},{3,2},{4,3},{5,4},{6,5},{7,6},{0,7},{9,8},{10,9},{11,1... | collective-permute-start | bytes 196616 | tf_op jit(solution)/shard_map/ppermute | solution.py:22
  70.8 1.9 collective-permute-start.2
  72.7 5.1 %collective-permute-start.5 = (bf16[128,256]{1,0:T(8,128)(2,1)S(1)}, bf16[128,256]{1,0:T(8,128)(2,1)S(1)}, u32[]{:S(2)}, u32[]{:S(2)}) collective-permute-start(bf16[128,256]{1,0:T(8,128)(2,1)S(1)} %collective-permute-done.4), channel_id=1, source_target_pairs={{1,0},{2,1},{3,2},{4,3},{5,4},{6,5},{7,6},{0,7},{9,8},{10,9},{11,1... | collective-permute-start | bytes 196616 | tf_op jit(solution)/shard_map/ppermute | solution.py:22
  80.1 5.1 %collective-permute-start.6 = (bf16[128,256]{1,0:T(8,128)(2,1)S(1)}, bf16[128,256]{1,0:T(8,128)(2,1)S(1)}, u32[]{:S(2)}, u32[]{:S(2)}) collective-permute-start(bf16[128,256]{1,0:T(8,128)(2,1)S(1)} %collective-permute-done.5), channel_id=1, source_target_pairs={{1,0},{2,1},{3,2},{4,3},{5,4},{6,5},{7,6},{0,7},{9,8},{10,9},{11,1... | collective-permute-start | bytes 196616 | tf_op jit(solution)/shard_map/ppermute | solution.py:22
  91.7 3.7 %all_to_all.32 = bf16[64,6,2048]{2,1,0:T(8,128)(2,1)} reshape(bf16[384,2048]{1,0:T(8,128)(2,1)} %convolution_convert_fusion.2) | data formatting | bytes 3145728 | tf_op jit(solution)/shard_map/all_to_all | solution.py:75
  95.4 10.2 %all-to-all-done.2 = bf16[64,6,2048]{2,1,0:T(8,128)(2,1)S(1)} async-done(((bf16[64,6,2048]{2,1,0:T(8,128)(2,1)}), bf16[64,6,2048]{2,1,0:T(8,128)(2,1)S(1)}, u32[]{:S(2)}, u32[]{:S(2)}) %all-to-all-start.2) | async-done | bytes 1572896 | tf_op jit(solution)/shard_map/all_to_all | solution.py:76
  105.6 7.7 %all-to-all-start = ((bf16[64,6,2048]{2,1,0:T(8,128)(2,1)}), bf16[64,6,2048]{2,1,0:T(8,128)(2,1)}, u32[]{:S(2)}, u32[]{:S(2)}) async-start(bf16[64,6,2048]{2,1,0:T(8,128)(2,1)} %all_to_all.32), calls=%async_computation | async-start | bytes 4194304 | tf_op jit(solution)/shard_map/all_to_all | solution.py:75
  114.8 48.0 %all-to-all-done = bf16[64,6,2048]{2,1,0:T(8,128)(2,1)} async-done(((bf16[64,6,2048]{2,1,0:T(8,128)(2,1)}), bf16[64,6,2048]{2,1,0:T(8,128)(2,1)}, u32[]{:S(2)}, u32[]{:S(2)}) %all-to-all-start) | async-done | bytes 1572896 | tf_op jit(solution)/shard_map/all_to_all | solution.py:75
  162.7 2.6 all_to_all.34
  172.6 7.5 %all-to-all-start.3 = ((bf16[64,6,2048]{2,1,0:T(8,128)(2,1)}), bf16[64,6,2048]{2,1,0:T(8,128)(2,1)S(1)}, u32[]{:S(2)}, u32[]{:S(2)}) async-start(bf16[64,6,2048]{2,1,0:T(8,128)(2,1)} %all_to_all.41), calls=%async_computation.4 | async-start | bytes 4194304 | tf_op jit(solution)/shard_map/all_to_all | solution.py:127
  181.7 2.8 convolution_convert_fusion
  184.6 3.7 %all_to_all.35 = bf16[64,6,2048]{2,1,0:T(8,128)(2,1)} reshape(bf16[384,2048]{1,0:T(8,128)(2,1)} %convolution_convert_fusion) | data formatting | bytes 3145728 | tf_op jit(solution)/shard_map/all_to_all | solution.py:126
  188.2 41.4 %all-to-all-done.3 = bf16[64,6,2048]{2,1,0:T(8,128)(2,1)S(1)} async-done(((bf16[64,6,2048]{2,1,0:T(8,128)(2,1)}), bf16[64,6,2048]{2,1,0:T(8,128)(2,1)S(1)}, u32[]{:S(2)}, u32[]{:S(2)}) %all-to-all-start.3) | async-done | bytes 1572896 | tf_op jit(solution)/shard_map/all_to_all | solution.py:127
  231.0 7.5 %all-to-all-start.1 = ((bf16[64,6,2048]{2,1,0:T(8,128)(2,1)}), bf16[64,6,2048]{2,1,0:T(8,128)(2,1)S(1)}, u32[]{:S(2)}, u32[]{:S(2)}) async-start(bf16[64,6,2048]{2,1,0:T(8,128)(2,1)} %all_to_all.35), calls=%async_computation.1 | async-start | bytes 4194304 | tf_op jit(solution)/shard_map/all_to_all | solution.py:126
  244.0 3.7 %all_to_all.43 = bf16[384,2048]{1,0:T(8,128)(2,1)} reshape(bf16[64,6,2048]{2,1,0:T(8,128)(2,1)} %copy-done.1) | data formatting | bytes 3145728 | tf_op jit(solution)/shard_map/all_to_all | solution.py:127
  247.7 3.3 convolution_add_fusion
  251.1 2.3 fusion.25
  253.3 34.7 %all-to-all-done.1 = bf16[64,6,2048]{2,1,0:T(8,128)(2,1)S(1)} async-done(((bf16[64,6,2048]{2,1,0:T(8,128)(2,1)}), bf16[64,6,2048]{2,1,0:T(8,128)(2,1)S(1)}, u32[]{:S(2)}, u32[]{:S(2)}) %all-to-all-start.1) | async-done | bytes 1572896 | tf_op jit(solution)/shard_map/all_to_all | solution.py:126
  289.5 3.8 %convolution_add_fusion.2 = f32[128,2048]{1,0:T(8,128)} fusion(f32[128,2048]{1,0:T(8,128)} %fusion.25, bf16[384,2048]{1,0:T(8,128)(2,1)} %all_to_all.37, f32[384]{0:T(512)S(1)} %select_reduce_fusion, pred[384,128]{1,0:T(8,128)(4,1)S(1)} %copy-done.9), kind=kOutput, calls=%fused_computation.7 | convolution fusion | flops 1208369152 | bytes 3720704 | tf_op jit(solution)/shard_map/st,sd->td/dot_general | solution.py:129
  294.8 40.0 %reduce-scatter.3.cloned.1.call-done = f32[128,256]{1,0:T(8,128)} async-done(((f32[128,2048]{1,0:T(8,128)}), f32[128,256]{1,0:T(8,128)}) %reduce-scatter.3.cloned.1.call-update) | async-done | bytes 131088 | tf_op jit(solution)/shard_map/reduce_scatter | solution.py:144
  (100 shorter events, 40.2 us)
Async XLA Ops:
  7.2 160.8 %copy-start = (bf16[1,176,2048]{2,1,0:T(8,128)(2,1)S(1)}, bf16[1,176,2048]{2,1,0:T(8,128)(2,1)}, u32[]{:S(2)}) copy-start(bf16[1,176,2048]{2,1,0:T(8,128)(2,1)} %param.19) | copy-start | bytes 2162692
  7.2 4.6 %copy-start.19 = (f32[128,6]{0,1:T(8,128)S(1)}, f32[128,6]{0,1:T(8,128)}, u32[]{:S(2)}) copy-start(f32[128,6]{0,1:T(8,128)} %param.13) | copy-start | bytes 9220
  7.2 4.9 %copy-start.15 = (bf16[128,256]{1,0:T(8,128)(2,1)S(1)}, bf16[128,256]{1,0:T(8,128)(2,1)}, u32[]{:S(2)}) copy-start(bf16[128,256]{1,0:T(8,128)(2,1)} %param.11) | copy-start | bytes 196612
  11.8 78.1 %copy-start.8 = (pred[384,128]{1,0:T(8,128)(4,1)}, pred[384,128]{1,0:T(8,128)(4,1)S(1)}, u32[]{:S(2)}) copy-start(pred[384,128]{1,0:T(8,128)(4,1)S(1)} %fusion.2) | copy-start | bytes 147460
  42.0 14.0 %copy-start.16 = (bf16[128,256]{1,0:T(8,128)(2,1)S(1)}, bf16[128,256]{1,0:T(8,128)(2,1)}, u32[]{:S(2)}) copy-start(bf16[128,256]{1,0:T(8,128)(2,1)} %param.10) | copy-start | bytes 196612
  42.0 63.6 %all-to-all-start.2 = ((bf16[64,6,2048]{2,1,0:T(8,128)(2,1)}), bf16[64,6,2048]{2,1,0:T(8,128)(2,1)S(1)}, u32[]{:S(2)}, u32[]{:S(2)}) async-start(bf16[64,6,2048]{2,1,0:T(8,128)(2,1)} %all_to_all.38), calls=%async_computation.3 | async-start | bytes 4194304 | tf_op jit(solution)/shard_map/all_to_all | solution.py:76
  56.0 7.4 %collective-permute-start = (bf16[128,256]{1,0:T(8,128)(2,1)S(1)}, bf16[128,256]{1,0:T(8,128)(2,1)S(1)}, u32[]{:S(2)}, u32[]{:S(2)}) collective-permute-start(bf16[128,256]{1,0:T(8,128)(2,1)S(1)} %copy-done.16), channel_id=1, source_target_pairs={{0,1},{1,2},{2,3},{3,4},{4,5},{5,6},{6,7},{7,0},{8,9},{9,10},{10,1... | collective-permute-start | bytes 196616 | tf_op jit(solution)/shard_map/ppermute | solution.py:20
  63.4 7.4 %collective-permute-start.1 = (bf16[128,256]{1,0:T(8,128)(2,1)S(1)}, bf16[128,256]{1,0:T(8,128)(2,1)S(1)}, u32[]{:S(2)}, u32[]{:S(2)}) collective-permute-start(bf16[128,256]{1,0:T(8,128)(2,1)S(1)} %collective-permute-done), channel_id=1, source_target_pairs={{0,1},{1,2},{2,3},{3,4},{4,5},{5,6},{6,7},{7,0},{8,9},{9,10},{10,1... | collective-permute-start | bytes 196616 | tf_op jit(solution)/shard_map/ppermute | solution.py:20
  65.3 7.4 %collective-permute-start.4 = (bf16[128,256]{1,0:T(8,128)(2,1)S(1)}, bf16[128,256]{1,0:T(8,128)(2,1)S(1)}, u32[]{:S(2)}, u32[]{:S(2)}) collective-permute-start(bf16[128,256]{1,0:T(8,128)(2,1)S(1)} %copy-done.16), channel_id=1, source_target_pairs={{1,0},{2,1},{3,2},{4,3},{5,4},{6,5},{7,6},{0,7},{9,8},{10,9},{11,1... | collective-permute-start | bytes 196616 | tf_op jit(solution)/shard_map/ppermute | solution.py:22
  70.8 14.5 %copy-start.18 = (bf16[128,256]{1,0:T(8,128)(2,1)}, bf16[128,256]{1,0:T(8,128)(2,1)S(1)}, u32[]{:S(2)}) copy-start(bf16[128,256]{1,0:T(8,128)(2,1)S(1)} %collective-permute-done.1) | copy-start | bytes 196612
  70.8 7.4 %collective-permute-start.2 = (bf16[128,256]{1,0:T(8,128)(2,1)S(1)}, bf16[128,256]{1,0:T(8,128)(2,1)S(1)}, u32[]{:S(2)}, u32[]{:S(2)}) collective-permute-start(bf16[128,256]{1,0:T(8,128)(2,1)S(1)} %collective-permute-done.1), channel_id=1, source_target_pairs={{0,1},{1,2},{2,3},{3,4},{4,5},{5,6},{6,7},{7,0},{8,9},{9,10},{10,1... | collective-permute-start | bytes 196616 | tf_op jit(solution)/shard_map/ppermute | solution.py:20
  72.7 12.5 %copy-start.17 = (bf16[128,256]{1,0:T(8,128)(2,1)}, bf16[128,256]{1,0:T(8,128)(2,1)S(1)}, u32[]{:S(2)}) copy-start(bf16[128,256]{1,0:T(8,128)(2,1)S(1)} %collective-permute-done.4) | copy-start | bytes 196612
  72.7 7.3 %collective-permute-start.5 = (bf16[128,256]{1,0:T(8,128)(2,1)S(1)}, bf16[128,256]{1,0:T(8,128)(2,1)S(1)}, u32[]{:S(2)}, u32[]{:S(2)}) collective-permute-start(bf16[128,256]{1,0:T(8,128)(2,1)S(1)} %collective-permute-done.4), channel_id=1, source_target_pairs={{1,0},{2,1},{3,2},{4,3},{5,4},{6,5},{7,6},{0,7},{9,8},{10,9},{11,1... | collective-permute-start | bytes 196616 | tf_op jit(solution)/shard_map/ppermute | solution.py:22
  78.1 7.4 %collective-permute-start.3 = (bf16[128,256]{1,0:T(8,128)(2,1)S(1)}, bf16[128,256]{1,0:T(8,128)(2,1)S(1)}, u32[]{:S(2)}, u32[]{:S(2)}) collective-permute-start(bf16[128,256]{1,0:T(8,128)(2,1)S(1)} %collective-permute-done.2), channel_id=1, source_target_pairs={{0,1},{1,2},{2,3},{3,4},{4,5},{5,6},{6,7},{7,0},{8,9},{9,10},{10,1... | collective-permute-start | bytes 196616 | tf_op jit(solution)/shard_map/ppermute | solution.py:20
  80.1 7.2 %collective-permute-start.6 = (bf16[128,256]{1,0:T(8,128)(2,1)S(1)}, bf16[128,256]{1,0:T(8,128)(2,1)S(1)}, u32[]{:S(2)}, u32[]{:S(2)}) collective-permute-start(bf16[128,256]{1,0:T(8,128)(2,1)S(1)} %collective-permute-done.5), channel_id=1, source_target_pairs={{1,0},{2,1},{3,2},{4,3},{5,4},{6,5},{7,6},{0,7},{9,8},{10,9},{11,1... | collective-permute-start | bytes 196616 | tf_op jit(solution)/shard_map/ppermute | solution.py:22
  105.6 57.2 %all-to-all-start = ((bf16[64,6,2048]{2,1,0:T(8,128)(2,1)}), bf16[64,6,2048]{2,1,0:T(8,128)(2,1)}, u32[]{:S(2)}, u32[]{:S(2)}) async-start(bf16[64,6,2048]{2,1,0:T(8,128)(2,1)} %all_to_all.32), calls=%async_computation | async-start | bytes 4194304 | tf_op jit(solution)/shard_map/all_to_all | solution.py:75
  172.6 57.1 %all-to-all-start.3 = ((bf16[64,6,2048]{2,1,0:T(8,128)(2,1)}), bf16[64,6,2048]{2,1,0:T(8,128)(2,1)S(1)}, u32[]{:S(2)}, u32[]{:S(2)}) async-start(bf16[64,6,2048]{2,1,0:T(8,128)(2,1)} %all_to_all.41), calls=%async_computation.4 | async-start | bytes 4194304 | tf_op jit(solution)/shard_map/all_to_all | solution.py:127
  231.0 57.1 %all-to-all-start.1 = ((bf16[64,6,2048]{2,1,0:T(8,128)(2,1)}), bf16[64,6,2048]{2,1,0:T(8,128)(2,1)S(1)}, u32[]{:S(2)}, u32[]{:S(2)}) async-start(bf16[64,6,2048]{2,1,0:T(8,128)(2,1)} %all_to_all.35), calls=%async_computation.1 | async-start | bytes 4194304 | tf_op jit(solution)/shard_map/all_to_all | solution.py:126
  238.5 54.8 %reduce-scatter.5.cloned.1.call-start = ((), (), s32[]{:S(2)}) async-start(), calls=%async_computation.7 | async-start | bytes 1179648 | tf_op jit(solution)/shard_map/reduce_scatter | solution.py:145
  238.5 3.7 %copy-start.3 = (bf16[176,2048]{1,0:T(8,128)(2,1)S(1)}, bf16[176,2048]{1,0:T(8,128)(2,1)}, u32[]{:S(2)}) copy-start(bf16[176,2048]{1,0:T(8,128)(2,1)} %param.14) | copy-start | bytes 2162692
  240.1 2.5 copy-start.7
  247.7 3.3 copy-start.5
  251.0 83.8 %reduce-scatter.3.cloned.1.call-start = ((), (), s32[]{:S(2)}) async-start(), calls=%async_computation.6 | async-start | bytes 1179648 | tf_op jit(solution)/shard_map/reduce_scatter | solution.py:144
  253.3 36.2 %copy-start.9 = (pred[384,128]{1,0:T(8,128)(4,1)S(1)}, pred[384,128]{1,0:T(8,128)(4,1)}, u32[]{:S(2)}) copy-start(pred[384,128]{1,0:T(8,128)(4,1)} %copy-done.8) | copy-start | bytes 147460
  (9 other events, 12.8 us)
Sparse Core Ops, SparseCore 0:
  251.1 40.6 reduce-scatter.4
  294.6 40.1 reduce-scatter.2
